TPU v7x, 512 devices: a whole 4x8x8 slice. The times are simulated.
512 devices in a mesh: replica: 8 (over y), shard: 64 (over z, x, core).
Axes of the slice: x: 4, y: 8, z: 8, core: 2. Of those that a mesh axis runs over, the one named last changes fastest.
Arguments:
- hidden_states: bfloat16 [131072, 7168], P(('replica', 'shard')), may hold values from -6 to 6
- latent_grad: bfloat16 [131072, 512], P(('replica', 'shard')), may hold values from -0.078125 to 0.078125
- left_factor: float32 [128, 256, 256], P('shard', 'replica'), may hold values from -2 to 45, as said below
- right_factor: float32 [128, 256, 256], P('shard', 'replica'), may hold values from -2 to 45, as said below
- left_root: bfloat16 [128, 256, 256], P('shard'), may hold values from -1 to 4, as said below
- right_root: bfloat16 [128, 256, 256], P('shard'), may hold values from -1 to 4, as said below
- block_owner: int32 [56], replicated, may hold values from 0 to 63, as said below
- block_slot: int32 [56], replicated, may hold values from 0 to 1, as said below
Outputs:
- new_left: float32 [128, 256, 256], P('shard', 'replica')
- new_right: float32 [128, 256, 256], P('shard', 'replica')
- update: float32 [2, 256, 7168], P(None, 'shard')
Inputs may be any that keep to these rules, and one draw needn't show every extreme that they name: `block_owner`: no owner holds more than 2 blocks, and some owner holds exactly 2. `block_slot`: no two blocks have both the same owner and the same slot. `left_factor`: Symmetric. `right_factor`: Symmetric. `left_root`: Symmetric. `right_root`: Symmetric.
All inputs are finite; a program needn't handle non-finite values.
Results may differ from a plain program's by a relative error of at most 0.005.
Values may be sent and summed in bfloat16 or wider, within the bound.
A program may use at most 64 MiB of HBM per device.

v0:
```python
import jax
import jax.numpy as jnp
from jax import lax
from jax.sharding import PartitionSpec as P

D = 7168
LAT = 512
BS = 256


decay_rate = 0.95
epsilon = 1e-06


def from_everyone(shard, axis):
    peers = lax.axis_size(axis)
    return lax.all_to_all(
        jnp.broadcast_to(shard[None], (peers, *shard.shape)), axis, 0, 0, tiled=True
    )


def of_everyone(shard, axis):
    everything = from_everyone(shard, axis)
    return jnp.sum(everything, axis=0)


def local(
    hidden_states,
    latent_grad,
    left_factor,
    right_factor,
    left_root,
    right_root,
    block_owner,
    block_slot,
):
    shards = lax.axis_size("shard")
    replicas = lax.axis_size("replica")
    strip_rows = BS // shards
    row_blocks = LAT // BS
    col_blocks = D // BS
    block_count = row_blocks * col_blocks
    capacity = left_root.shape[0]
    high = lax.Precision.HIGHEST
    tokens_here = latent_grad.shape[0]
    reordered = (
        latent_grad.reshape(tokens_here, row_blocks, shards, strip_rows)
        .transpose(0, 2, 1, 3)
        .reshape(tokens_here, LAT)
    )
    partial_value = jnp.einsum(
        "tl,td->ld", reordered, hidden_states, preferred_element_type=jnp.float32
    ).astype(jnp.bfloat16)
    pieces = partial_value.reshape(shards, row_blocks * strip_rows, D)
    received = lax.all_to_all(pieces, "shard", split_axis=0, concat_axis=0, tiled=True)
    shard_total = jnp.sum(received, axis=0, dtype=jnp.float32)
    gradient_slab = of_everyone(shard_total, "replica")
    strips = (
        gradient_slab.reshape(row_blocks, strip_rows, col_blocks, BS)
        .transpose(0, 2, 1, 3)
        .reshape(block_count, strip_rows * BS)
    )
    flat_slot = block_owner * capacity + block_slot
    owners_iota = lax.broadcasted_iota(jnp.int32, (shards * capacity, block_count), 0)
    matcher = (owners_iota == flat_slot[None, :]).astype(jnp.float32)
    outgoing = jnp.dot(matcher, strips, precision=high, preferred_element_type=jnp.float32).reshape(
        shards, capacity, strip_rows, BS
    )
    blocks = (
        lax.all_to_all(
            outgoing.astype(jnp.bfloat16), "shard", split_axis=0, concat_axis=2, tiled=True
        )
        .astype(outgoing.dtype)
        .reshape(capacity, BS, BS)
    )
    part_rows = BS // replicas
    row_start = lax.axis_index("replica") * part_rows
    rows_part = lax.dynamic_slice_in_dim(blocks, row_start, part_rows, 1)
    cols_part = lax.dynamic_slice_in_dim(blocks, row_start, part_rows, 2)
    new_left = decay_rate * left_factor + (1.0 - decay_rate) * jnp.einsum(
        "cik,cjk->cij", rows_part, blocks, precision=high
    )
    new_right = decay_rate * right_factor + (1.0 - decay_rate) * jnp.einsum(
        "cki,ckj->cij", cols_part, blocks, precision=high
    )
    rounded = blocks.astype(jnp.bfloat16)
    half_product = jnp.einsum(
        "cik,ckj->cij", left_root, rounded, preferred_element_type=jnp.float32
    ).astype(jnp.bfloat16)
    shaped = jnp.einsum(
        "cik,ckj->cij", half_product, right_root, preferred_element_type=jnp.float32
    )
    grad_scale = jnp.sqrt(jnp.mean(blocks * blocks, axis=(1, 2)))
    shaped_scale = jnp.sqrt(jnp.mean(shaped * shaped, axis=(1, 2)) + epsilon)
    update_blocks = shaped * (grad_scale / shaped_scale)[:, None, None]
    returned = lax.all_to_all(
        update_blocks.reshape(capacity, shards, strip_rows, BS),
        "shard",
        split_axis=1,
        concat_axis=1,
        tiled=True,
    )
    pick_iota = lax.broadcasted_iota(jnp.int32, (block_count, capacity * shards), 1)
    slot_key = block_slot * shards + block_owner
    selector = (pick_iota == slot_key[:, None]).astype(jnp.float32)
    chosen_rows = jnp.dot(
        selector,
        returned.reshape(capacity * shards, strip_rows * BS),
        precision=high,
        preferred_element_type=jnp.float32,
    )
    update = (
        chosen_rows.reshape(row_blocks, col_blocks, strip_rows, BS)
        .transpose(0, 2, 1, 3)
        .reshape(row_blocks, strip_rows, D)
    )
    return (new_left, new_right, update)


def solution(mesh):
    placed = (
        P(("replica", "shard"), None),
        P(("replica", "shard"), None),
        P("shard", "replica", None),
        P("shard", "replica", None),
        P("shard", None, None),
        P("shard", None, None),
        P(),
        P(),
    )
    return jax.shard_map(
        local,
        mesh=mesh,
        in_specs=placed,
        out_specs=(
            P("shard", "replica", None),
            P("shard", "replica", None),
            P(None, "shard", None),
        ),
        check_vma=False,
    )
```

profile of v0, /device:TPU:1, one launch (start us, length us, event | category | flops | bytes accessed | tf_op | source)
XLA Modules:
  0.0 285.7 jit_solution(1103719108993614763)
XLA Ops:
  0.6 0.0 copy-start
  0.6 1.1 copy.51
  1.8 0.1 reshape.107
  1.8 0.1 copy.52
  1.9 0.1 reshape.108
  2.0 4.1 %fusion = bf16[64,8,7168]{2,1,0:T(8,128)(2,1)S(1)} fusion(bf16[256,512]{0,1:T(8,128)(2,1)S(1)} %reshape.108, bf16[256,7168]{1,0:T(8,128)(2,1)} %param.8), kind=kOutput, calls=%fused_computation.2 | convolution fusion | flops 1882718208 | bytes 11272192 | tf_op jit(solution)/shard_map/tl,td->ld/dot_general | solution.py:51
  6.1 177.3 %all_to_all.30 = bf16[64,8,7168]{2,1,0:T(8,128)(2,1)S(1)} all-to-all(bf16[64,8,7168]{2,1,0:T(8,128)(2,1)S(1)} %fusion), channel_id=1, replica_groups=mesh['replica'=8,'shard'=64] {'shard'}, dimensions={0} | all-to-all | bytes 14680064 | tf_op jit(solution)/shard_map/all_to_all | solution.py:55
  183.5 0.0 copy-start.4
  183.5 0.0 copy-start.5
  183.5 1.2 convert_reduce_fusion
  184.7 0.0 copy-start.1
  184.7 1.4 broadcast_in_dim.2
  186.1 0.0 copy-start.2
  186.1 0.0 copy-start.3
  186.1 7.0 %all-to-all-start.1 = ((f32[8,8,7168]{2,1,0:T(8,128)}), f32[8,8,7168]{2,1,0:T(8,128)S(1)}, u32[]{:S(2)}, u32[]{:S(2)}) async-start(f32[8,8,7168]{2,1,0:T(8,128)} %broadcast_in_dim.2), calls=%async_computation.1 | async-start | bytes 3670016 | tf_op jit(solution)/shard_map/all_to_all | solution.py:17
  193.0 0.0 copy-done.4
  193.0 0.0 copy-done.5
  193.1 43.1 %all-to-all-done.1 = f32[8,8,7168]{2,1,0:T(8,128)S(1)} async-done(((f32[8,8,7168]{2,1,0:T(8,128)}), f32[8,8,7168]{2,1,0:T(8,128)S(1)}, u32[]{:S(2)}, u32[]{:S(2)}) %all-to-all-start.1) | async-done | bytes 1835040 | tf_op jit(solution)/shard_map/all_to_all | solution.py:17
  236.2 0.1 reduce_sum.37
  236.4 0.2 copy.53
  236.5 0.5 convolution_convert_fusion.2
  237.0 0.2 copy.55
  237.2 22.1 %all_to_all.31 = bf16[64,2,4,256]{3,2,1,0:T(4,128)(2,1)S(1)} all-to-all(bf16[64,2,4,256]{3,2,1,0:T(4,128)(2,1)S(1)} %copy.55), channel_id=1, replica_groups=mesh['replica'=8,'shard'=64] {'shard'}, dimensions={0} | all-to-all | bytes 524288 | tf_op jit(solution)/shard_map/all_to_all | solution.py:70
  259.3 0.2 copy.56
  259.5 0.2 copy.59
  259.7 0.0 copy-done
  259.7 0.0 copy-done.1
  259.7 0.6 multiply_reduce_fusion
  260.3 0.3 multiply_reduce_fusion.1
  260.6 0.1 broadcast_multiply_fusion
  260.7 0.1 reshape.113
  260.9 0.8 copy.63
  261.7 4.7 %all-to-all-start.3 = ((f32[2,64,4,256]{3,2,0,1:T(4,128)}), f32[2,64,4,256]{3,2,0,1:T(4,128)S(1)}, u32[]{:S(2)}, u32[]{:S(2)}) async-start(f32[2,64,4,256]{3,2,0,1:T(4,128)} %copy.63), calls=%async_computation.3 | async-start | bytes 1048576 | tf_op jit(solution)/shard_map/all_to_all | solution.py:96
  266.4 0.1 iota_compare_fusion
  266.6 0.0 copy-done.2
  266.6 0.8 fusion.3
  267.4 0.0 copy-done.3
  267.4 0.8 fusion.2
  268.2 16.0 %all-to-all-done.3 = f32[2,64,4,256]{3,2,0,1:T(4,128)S(1)} async-done(((f32[2,64,4,256]{3,2,0,1:T(4,128)}), f32[2,64,4,256]{3,2,0,1:T(4,128)S(1)}, u32[]{:S(2)}, u32[]{:S(2)}) %all-to-all-start.3) | async-done | bytes 524320 | tf_op jit(solution)/shard_map/all_to_all | solution.py:96
  284.2 0.1 copy.71
  284.3 0.2 copy.65
  284.5 0.4 convolution_bitcast_fusion
  284.9 0.8 reshape.115
  (7 shorter events, 0.1 us)
Async XLA Ops:
  0.6 259.1 %copy-start = (bf16[2,256,256]{2,1,0:T(8,128)(2,1)S(1)}, bf16[2,256,256]{2,1,0:T(8,128)(2,1)}, u32[]{:S(2)}) copy-start(bf16[2,256,256]{2,1,0:T(8,128)(2,1)} %param.13) | copy-start | bytes 786436
  183.5 9.5 %copy-start.4 = (s32[56]{0:T(128)S(1)}, s32[56]{0:T(128)}, u32[]{:S(2)}) copy-start(s32[56]{0:T(128)} %param.14) | copy-start | bytes 676
  183.5 9.6 %copy-start.5 = (s32[56]{0:T(128)S(1)}, s32[56]{0:T(128)}, u32[]{:S(2)}) copy-start(s32[56]{0:T(128)} %param.15) | copy-start | bytes 676
  184.7 75.1 %copy-start.1 = (bf16[2,256,256]{2,1,0:T(8,128)(2,1)S(1)}, bf16[2,256,256]{2,1,0:T(8,128)(2,1)}, u32[]{:S(2)}) copy-start(bf16[2,256,256]{2,1,0:T(8,128)(2,1)} %param.12) | copy-start | bytes 786436
  186.1 80.5 %copy-start.2 = (f32[2,32,256]{2,1,0:T(8,128)S(1)}, f32[2,32,256]{2,1,0:T(8,128)}, u32[]{:S(2)}) copy-start(f32[2,32,256]{2,1,0:T(8,128)} %param.11) | copy-start | bytes 196612
  186.1 81.3 %copy-start.3 = (f32[2,32,256]{2,1,0:T(8,128)S(1)}, f32[2,32,256]{2,1,0:T(8,128)}, u32[]{:S(2)}) copy-start(f32[2,32,256]{2,1,0:T(8,128)} %param.10) | copy-start | bytes 196612
  186.1 50.1 %all-to-all-start.1 = ((f32[8,8,7168]{2,1,0:T(8,128)}), f32[8,8,7168]{2,1,0:T(8,128)S(1)}, u32[]{:S(2)}, u32[]{:S(2)}) async-start(f32[8,8,7168]{2,1,0:T(8,128)} %broadcast_in_dim.2), calls=%async_computation.1 | async-start | bytes 3670016 | tf_op jit(solution)/shard_map/all_to_all | solution.py:17
  261.7 22.4 %all-to-all-start.3 = ((f32[2,64,4,256]{3,2,0,1:T(4,128)}), f32[2,64,4,256]{3,2,0,1:T(4,128)S(1)}, u32[]{:S(2)}, u32[]{:S(2)}) async-start(f32[2,64,4,256]{3,2,0,1:T(4,128)} %copy.63), calls=%async_computation.3 | async-start | bytes 1048576 | tf_op jit(solution)/shard_map/all_to_all | solution.py:96
where the time goes:
time: 286 us
  blocking collectives  199 us (70%)
  waiting for transfers between devices  59.1 us (21%)
  starting transfers between devices  11.7 us (4%)
  matrix products  7.25 us (3%)
  local copies, waits for them, and re-layouts  5.69 us (2%)
    all_to_all x1, blocking collectives, local(): lax.all_to_all(pieces, 'shard', split_axis=0, concat_axis=0, tiled=True)  177 us
    all_to_all x1, waiting for transfers between devices, from_everyone(): lax.all_to_all(jnp.broadcast_to(shard[None], (peers, *shard.shape)), axis...  43.1 us
    all_to_all x1, blocking collectives, local(): lax.all_to_all(outgoing.astype(jnp.bfloat16), 'shard', split_axis=0, conc...  22.1 us
    all_to_all x1, waiting for transfers between devices, local(): lax.all_to_all(update_blocks.reshape(capacity, shards, strip_rows, BS), '...  16 us
    all_to_all x1, starting transfers between devices, from_everyone(): lax.all_to_all(jnp.broadcast_to(shard[None], (peers, *shard.shape)), axis...  6.95 us
  transfers between devices with their start and end apart: 2, of which 2 were waited for; matrix products, arithmetic and copies ran while one was open for 1% of the time, Pallas kernels for 0%

commit v1 on v0

v1 whole, which is shorter than its diff:
```python
import functools

import jax
import jax.numpy as jnp
from jax import lax
from jax.experimental import pallas as pl
from jax.experimental.pallas import tpu as pltpu
from jax.sharding import PartitionSpec as P

D = 7168
LAT = 512
BS = 256
TOK = 256
NX, NY, NZ = 4, 8, 8
NT = 8
HALF = 128
DECAY = 0.95
EPS = 1e-06

PARTS = (
    (0, "m", 5, 9),
    (1, "m", 19, 9),
    (0, "x", 0, 5),
    (1, "x", 14, 5),
)
MESH = pl.DeviceIdType.MESH
F32 = jnp.float32
BF16 = jnp.bfloat16


def chain_shapes():
    shapes = {}
    for p, (_, first, _, nj) in enumerate(PARTS):
        for stage in range(2):
            over = first if stage == 0 else ("x" if first == "m" else "m")
            n = NX if over == "x" else 8
            rows = LAT // n if stage == 0 else 16
            for step in range(n // 2):
                for d in range(2):
                    shapes[(p, stage, d, step)] = (rows // 2 if step == 0 else rows, nj * HALF)
    return shapes


CHAIN = chain_shapes()
KEYS = tuple(CHAIN)
INDEX = {key: k for k, key in enumerate(KEYS)}


def one_hot(rows, cols, match):
    r = lax.broadcasted_iota(jnp.int32, (rows, cols), 0)
    c = lax.broadcasted_iota(jnp.int32, (rows, cols), 1)
    return jnp.where(match(r, c), 1.0, 0.0).astype(BF16)


def mm(a, b, ca=1, cb=0):
    return lax.dot_general(a, b, (((ca,), (cb,)), ((), ())), preferred_element_type=F32)


def kernel(hidden, latent, left_root, right_root, slots, ggl, ggr, upd, *scratch):
    n = len(KEYS)
    sends, recvs, scratch = scratch[:n], scratch[n : 2 * n], scratch[2 * n :]
    np_ = len(PARTS)
    hc, scratch = scratch[:np_], scratch[np_:]
    prod, scratch = scratch[:np_], scratch[np_:]
    mid, scratch = scratch[:np_], scratch[np_:]
    (lat, lt, s3, r3, s2z, z2, s2x, x2, yg, gf, s4z, z4, s4x, x4,
     hsem, csem_s, csem_r, s3sem, a2a) = scratch

    y = lax.axis_index("replica")
    s = lax.axis_index("shard")
    xc = s % 8
    c = s % 2
    x = (s // 2) % 4
    z = s // 8

    def dev(xx=None, yy=None, zz=None, xcc=None):
        q = xc if xcc is None else xcc
        if xx is not None:
            q = xx * 2 + c
        return (y if yy is None else yy, (z if zz is None else zz) * 8 + q)

    partner = dev(xcc=x * 2 + (1 - c))

    def own_copies(p):
        _, _, j0, nj = PARTS[p]
        return [
            pltpu.make_async_copy(
                hidden.at[:, pl.ds(pl.multiple_of((j0 + k) * BS + c * HALF, HALF), HALF)],
                hc[p].at[pl.ds(0, TOK), pl.ds(k * HALF, HALF)],
                hsem.at[0, p],
            )
            for k in range(nj)
        ]

    def far_copies(p):
        _, _, j0, nj = PARTS[p]
        return [
            pltpu.make_async_remote_copy(
                hidden.at[:, pl.ds(pl.multiple_of((j0 + k) * BS + (1 - c) * HALF, HALF), HALF)],
                hc[p].at[pl.ds(TOK, TOK), pl.ds(k * HALF, HALF)],
                hsem.at[1, p],
                hsem.at[2, p],
                device_id=partner,
                device_id_type=MESH,
            )
            for k in range(nj)
        ]

    def all_own(p):
        wide = PARTS[p][3] * HALF
        return pltpu.make_async_copy(
            hidden.at[:, pl.ds(0, wide)], hc[p].at[pl.ds(0, TOK), :], hsem.at[0, p]
        )

    def all_far(p):
        wide = PARTS[p][3] * HALF
        return pltpu.make_async_remote_copy(
            hidden.at[:, pl.ds(0, wide)], hc[p].at[pl.ds(TOK, TOK), :],
            hsem.at[1, p], hsem.at[2, p], device_id=partner, device_id_type=MESH,
        )

    own_lat = pltpu.make_async_copy(latent, lat.at[0], hsem.at[0, np_])
    far_lat = pltpu.make_async_remote_copy(
        latent, lat.at[1], hsem.at[1, np_], hsem.at[2, np_],
        device_id=partner, device_id_type=MESH,
    )
    own_lat.start()
    own = [own_copies(p) for p in range(np_)]
    far = [far_copies(p) for p in range(np_)]
    for p in range(np_):
        for k in own[p]:
            k.start()

    barrier = pltpu.get_barrier_semaphore()
    for d in range(1, 8):
        for to in (dev(yy=(y + d) % 8), dev(zz=(z + d) % 8), dev(xcc=(xc + d) % 8)):
            pl.semaphore_signal(barrier, inc=1, device_id=to, device_id_type=MESH)
    pl.semaphore_wait(barrier, 21)

    far_lat.start()
    for p in range(np_):
        for k in far[p]:
            k.start()

    perm_a = one_hot(LAT, LAT, lambda r, k: k == (r % 2) * BS + r // 2)
    perm_b = one_hot(
        LAT, LAT,
        lambda r, k: k == (r % 2) * BS + (r // 128) * 64 + ((r // 2) % 8) * 8 + (r // 16) % 8,
    )
    own_lat.wait()
    lt[0, :, 0:TOK] = mm(perm_a, lat[0], 1, 1).astype(BF16)
    lt[1, :, 0:TOK] = mm(perm_b, lat[0], 1, 1).astype(BF16)
    far_lat.wait_recv()
    lt[0, :, TOK : 2 * TOK] = mm(perm_a, lat[1], 1, 1).astype(BF16)
    lt[1, :, TOK : 2 * TOK] = mm(perm_b, lat[1], 1, 1).astype(BF16)

    def axis_of(p, stage):
        group, first, _, _ = PARTS[p]
        over = first if stage == 0 else ("x" if first == "m" else "m")
        if over == "x":
            return 4, x, lambda v: dev(xx=v)
        if group == 0:
            return 8, y, lambda v: dev(yy=v)
        return 8, z, lambda v: dev(zz=v)

    def copy_of(p, stage, d, step):
        num, me, at = axis_of(p, stage)
        k = INDEX[(p, stage, d, step)]
        to = (me + 1) % num if d == 0 else (me + num - 1) % num
        return pltpu.make_async_remote_copy(
            sends[k], recvs[k], csem_s.at[k], csem_r.at[k],
            device_id=at(to), device_id_type=MESH,
        )

    def own_rows(p, stage, chunk, piece):
        if stage == 0:
            if PARTS[p][1] == "x":
                start = chunk * 128 + piece * 16
            else:
                start = piece * 128 + chunk * 16
            return prod[p][pl.ds(pl.multiple_of(start, 16), 16), :]
        return mid[p][pl.ds(pl.multiple_of(chunk * 16 + piece * 8, 8), 8), :]

    def send_step(p, stage, step):
        num, me, _ = axis_of(p, stage)
        unit = 16 if stage == 0 else 8
        rows = (LAT // num if stage == 0 else 16) // unit
        for d in range(2):
            k = INDEX[(p, stage, d, step)]
            far_by = num // 2 - step
            chunk = (me + far_by) % num if d == 0 else (me + num - far_by) % num
            low, high = (0, rows) if step > 0 else ((0, rows // 2) if d == 0 else (rows // 2, rows))
            if step > 0:
                copy_of(p, stage, d, step - 1).wait_recv()
            prev = recvs[INDEX[(p, stage, d, step - 1)]] if step > 0 else None
            prev_low, prev_high = (low, high) if step > 1 else ((0, rows // 2) if d == 0 else (rows // 2, rows))

            def emit(a, b, add):
                @pl.loop(a, b)
                def _(i):
                    value = own_rows(p, stage, chunk, i)
                    if add:
                        value = value + prev[
                            pl.ds(pl.multiple_of((i - prev_low) * unit, unit), unit), :
                        ].astype(F32)
                    sends[k][pl.ds(pl.multiple_of((i - low) * unit, unit), unit), :] = value.astype(
                        sends[k].dtype
                    )

            if step == 0:
                emit(low, high, False)
            else:
                emit(prev_low, prev_high, True)
                if low < prev_low:
                    emit(low, prev_low, False)
                if prev_high < high:
                    emit(prev_high, high, False)
            copy_of(p, stage, d, step).start()

    def finish(p, stage):
        num, me, _ = axis_of(p, stage)
        unit = 16 if stage == 0 else 8
        rows = (LAT // num if stage == 0 else 16) // unit
        last = num // 2 - 1
        for d in range(2):
            copy_of(p, stage, d, last).wait_recv()
        up = recvs[INDEX[(p, stage, 0, last)]]
        down = recvs[INDEX[(p, stage, 1, last)]]
        if stage == 0:
            @pl.loop(0, rows)
            def _(i):
                at = pl.ds(pl.multiple_of(i * unit, unit), unit)
                mid[p][at, :] = (
                    own_rows(p, stage, me, i) + up[at, :].astype(F32) + down[at, :].astype(F32)
                )
        else:
            group, _, j0, nj = PARTS[p]
            for half in range(2):
                total = (
                    own_rows(p, stage, me, half)
                    + up[half * 8 : half * 8 + 8, :]
                    + down[half * 8 : half * 8 + 8, :]
                )
                for k in range(nj):
                    row = 2 * (j0 + k - 14 * group)
                    for t in range(4):
                        s3[group, half * 4 + t, row : row + 2, :] = total[
                            2 * t : 2 * t + 2, k * HALF : (k + 1) * HALF
                        ]

    for p in range(np_):
        all_own(p).wait()
        all_far(p).wait_recv()
        group, _, _, nj = PARTS[p]
        prod[p][...] = mm(lt[group], hc[p][...])
        send_step(p, 0, 0)

    ms = [p for p in range(np_) if PARTS[p][1] == "m"]
    xs = [p for p in range(np_) if PARTS[p][1] == "x"]
    s3[:, :, 28:32, :] = jnp.zeros((2, 8, 4, HALF), F32)
    for p in ms:
        send_step(p, 0, 1)
    for p in xs:
        send_step(p, 0, 1)
    for p in ms:
        send_step(p, 0, 2)
    for p in ms:
        send_step(p, 0, 3)
    for p in xs:
        finish(p, 0)
        send_step(p, 1, 0)
    for p in xs:
        send_step(p, 1, 1)
    for p in ms:
        finish(p, 0)
        send_step(p, 1, 0)
    for p in ms:
        send_step(p, 1, 1)
    for p in xs:
        send_step(p, 1, 2)
    for p in xs:
        send_step(p, 1, 3)
    for p in ms:
        finish(p, 1)
    for p in xs:
        finish(p, 1)

    def s3_copy(group, d):
        me = z if group == 0 else y
        to = (me + d) % 8
        return pltpu.make_async_remote_copy(
            s3.at[group, to], r3.at[group, d - 1],
            s3sem.at[0, group, d - 1], s3sem.at[1, group, d - 1],
            device_id=dev(zz=to) if group == 0 else dev(yy=to), device_id_type=MESH,
        )

    for group in range(2):
        for d in range(1, 8):
            s3_copy(group, d).start()
    pieces = []
    for group in range(2):
        total = s3[group, z if group == 0 else y]
        for d in range(1, 8):
            s3_copy(group, d).wait_recv()
            total = total + r3[group, d - 1]
        pieces.append(total)
    piece = jnp.concatenate(pieces, axis=0).astype(BF16)

    def exchange(k, src, dst, me, at, whole=False):
        return [
            pltpu.make_async_remote_copy(
                src if whole else src.at[(me + d) % 8],
                dst.at[me],
                a2a.at[k, 0, d - 1], a2a.at[k, 1, d - 1],
                device_id=at((me + d) % 8), device_id_type=MESH,
            )
            for d in range(1, 8)
        ]

    slot_row = slots[0:1, :]
    dispatch = jnp.where(
        lax.broadcasted_iota(jnp.int32, (128, 64), 0) == slot_row, 1.0, 0.0
    ).astype(BF16)
    s2z[...] = mm(dispatch, piece).astype(BF16).reshape(8, 16, HALF)
    ex = exchange(0, s2z, z2, z, lambda v: dev(zz=v))
    for k in ex:
        k.start()
    z2[z] = s2z[z]
    regroup = one_hot(
        128, 128, lambda o, i: i == (o % 8) * 16 + (o // 16) * 2 + (o // 8) % 2
    )
    for k in ex:
        k.wait_recv()
    s2x[...] = mm(regroup, z2[...].reshape(128, HALF)).astype(BF16).reshape(8, 16, HALF)
    ex2 = exchange(1, s2x, x2, xc, lambda v: dev(xcc=v))
    for k in ex2:
        k.start()
    x2[xc] = s2x[xc]
    for k in ex2:
        k.wait_recv()
    ex3 = exchange(2, x2, yg, y, lambda v: dev(yy=v), whole=True)
    for k in ex3:
        k.start()
    yg[y] = x2[...]
    for k in ex3:
        k.wait_recv()
    for yy in range(8):
        for q in range(8):
            both = yg[yy, q].astype(F32)
            row = (q // 2) * 64 + yy * 8
            for slot in range(2):
                gf[slot, row : row + 8, (q % 2) * HALF : (q % 2 + 1) * HALF] = both[
                    slot * 8 : slot * 8 + 8, :
                ]

    pick_rows = one_hot(64, BS, lambda r, k: k == r * 4 + y % 4)
    lane_half = pl.ds(pl.multiple_of((y // 4) * HALF, HALF), HALF)
    for slot in range(2):
        g = gf[slot]
        half = mm(left_root[slot], g.astype(BF16)).astype(BF16)
        shaped = mm(half, right_root[slot])
        grad_scale = jnp.sqrt(jnp.sum(g * g, keepdims=True) * (1.0 / (BS * BS)))
        shaped_scale = jnp.sqrt(jnp.sum(shaped * shaped, keepdims=True) * (1.0 / (BS * BS)) + EPS)
        chosen = mm(mm(pick_rows, half).astype(BF16), right_root[slot, :, lane_half])
        back = chosen * (grad_scale / shaped_scale)
        s4z[:, slot * 8 : slot * 8 + 8, :] = back.reshape(8, 8, HALF)
    ex4 = exchange(3, s4z, z4, z, lambda v: dev(zz=v))
    for k in ex4:
        k.start()
    z4[z] = s4z[z]

    rows_here = one_hot(32, BS, lambda r, k: k == r + y * 32)
    for slot in range(2):
        g = gf[slot].astype(BF16)
        ggl[slot] = mm(mm(rows_here, g).astype(BF16), g, 1, 1)
        ggr[slot] = mm(mm(rows_here, g, 1, 1).astype(BF16), g)

    for k in ex4:
        k.wait_recv()
    everything = z4[...].reshape(8, 2, 8, HALF)
    for q in range(8):
        s4x[q] = everything[:, :, q, :].reshape(16, HALF)
    ex5 = exchange(4, s4x, x4, xc, lambda v: dev(xcc=v))
    for k in ex5:
        k.start()
    x4[xc] = s4x[xc]
    owner = slot_row // 2
    back_slot = jnp.where(slot_row < 0, -1, (owner % 8) * 16 + (owner // 8) * 2 + slot_row % 2)
    picker = jnp.where(
        lax.broadcasted_iota(jnp.int32, (128, 64), 0) == back_slot, 1.0, 0.0
    )
    for k in ex5:
        k.wait_recv()
    upd[y] = lax.dot_general(
        picker, x4[...].reshape(128, HALF), (((0,), (0,)), ((), ())),
        precision=lax.Precision.HIGHEST, preferred_element_type=F32,
    )
    ex6 = exchange(5, upd.at[y], upd, y, lambda v: dev(yy=v), whole=True)
    for k in ex6:
        k.start()
    for k in ex6:
        k.wait_recv()

    far_lat.wait_send()
    for p in range(np_):
        all_far(p).wait_send()
    for key in KEYS:
        copy_of(*key).wait_send()
    for group in range(2):
        for d in range(1, 8):
            s3_copy(group, d).wait_send()
    for e in (ex, ex2, ex3, ex4, ex5, ex6):
        for k in e:
            k.wait_send()


def local(
    hidden_states,
    latent_grad,
    left_factor,
    right_factor,
    left_root,
    right_root,
    block_owner,
    block_slot,
):
    flat = (block_owner * 2 + block_slot).reshape(2, 2, 14).transpose(1, 2, 0).reshape(2, 28)
    slots = jnp.pad(flat, ((0, 0), (0, 4)), constant_values=-1).reshape(1, 64)
    slots = jnp.broadcast_to(slots, (8, 64))
    dtype_of = lambda key: BF16 if key[1] == 0 else F32
    bufs = [pltpu.VMEM(CHAIN[key], dtype_of(key)) for key in KEYS]
    scratch = bufs + bufs
    for width_of in (lambda w: ((2 * TOK, w), BF16), lambda w: ((LAT, w), F32)):
        scratch = scratch + [pltpu.VMEM(*width_of(part[3] * HALF)) for part in PARTS]
    scratch = scratch + [
        pltpu.VMEM((128 if part[1] == "x" else 64, part[3] * HALF), F32) for part in PARTS
    ]
    scratch = scratch + [
        pltpu.VMEM((2, TOK, LAT), BF16),
        pltpu.VMEM((2, LAT, 2 * TOK), BF16),
        pltpu.VMEM((2, 8, 32, HALF), F32),
        pltpu.VMEM((2, 7, 32, HALF), F32),
        pltpu.VMEM((8, 16, HALF), BF16),
        pltpu.VMEM((8, 16, HALF), BF16),
        pltpu.VMEM((8, 16, HALF), BF16),
        pltpu.VMEM((8, 16, HALF), BF16),
        pltpu.VMEM((8, 8, 16, HALF), BF16),
        pltpu.VMEM((2, BS, BS), F32),
        pltpu.VMEM((8, 16, HALF), F32),
        pltpu.VMEM((8, 16, HALF), F32),
        pltpu.VMEM((8, 16, HALF), F32),
        pltpu.VMEM((8, 16, HALF), F32),
        pltpu.SemaphoreType.DMA((3, len(PARTS) + 1)),
        pltpu.SemaphoreType.DMA((len(KEYS),)),
        pltpu.SemaphoreType.DMA((len(KEYS),)),
        pltpu.SemaphoreType.DMA((2, 2, 7)),
        pltpu.SemaphoreType.DMA((6, 2, 7)),
    ]
    vmem = pl.BlockSpec(memory_space=pltpu.VMEM)
    anywhere = pl.BlockSpec(memory_space=pl.ANY)
    ggl, ggr, upd = pl.pallas_call(
        kernel,
        out_shape=(
            jax.ShapeDtypeStruct((2, 32, BS), F32),
            jax.ShapeDtypeStruct((2, 32, BS), F32),
            jax.ShapeDtypeStruct((8, 64, HALF), F32),
        ),
        in_specs=[anywhere, anywhere, vmem, vmem, vmem],
        out_specs=(vmem, vmem, vmem),
        scratch_shapes=scratch,
        compiler_params=pltpu.CompilerParams(
            collective_id=0, has_side_effects=True, vmem_limit_bytes=56 * 1024 * 1024
        ),
    )(hidden_states, latent_grad, left_root, right_root, slots)
    new_left = DECAY * left_factor + (1.0 - DECAY) * ggl
    new_right = DECAY * right_factor + (1.0 - DECAY) * ggr
    update = (
        upd.reshape(2, 4, 2, 32, HALF)[:, :, :, :28]
        .reshape(2, 4, 2, 14, 2, HALF)
        .transpose(4, 1, 2, 3, 0, 5)
        .reshape(2, 4, D)
    )
    return (new_left, new_right, update)


def solution(mesh):
    placed = (
        P(("replica", "shard"), None),
        P(("replica", "shard"), None),
        P("shard", "replica", None),
        P("shard", "replica", None),
        P("shard", None, None),
        P("shard", None, None),
        P(),
        P(),
    )
    return jax.shard_map(
        local,
        mesh=mesh,
        in_specs=placed,
        out_specs=(
            P("shard", "replica", None),
            P("shard", "replica", None),
            P(None, "shard", None),
        ),
        check_vma=False,
    )
```

time: 286 us -> 103 us (0.36)
  blocking collectives: 199 us -> 0 us
  Pallas kernels: 0 us -> 96.2 us
  waiting for transfers between devices: 59.1 us -> 0 us
  starting transfers between devices: 11.7 us -> 0 us
  matrix products: 7.25 us -> 0 us
    all_to_all x2 -> x0, blocking collectives: 199 us -> none  [the longest x1 177 us: local(): lax.all_to_all(pieces, 'shard', split_axis=0, concat_axis=0, tiled=True)]
    pallas_call x0 -> x1, Pallas kernels: none -> 96.2 us  [local(): pl.pallas_call(kernel, out_shape=(jax.ShapeDtypeStruct((2, 32, BS), F32),...]
    all_to_all x2 -> x0, waiting for transfers between devices: 59.1 us -> none  [the longest x1 43.1 us: from_everyone(): lax.all_to_all(jnp.broadcast_to(shard[None], (peers, *shard.shape)), axis...]
    all_to_all x2 -> x0, starting transfers between devices: 11.7 us -> none  [the longest x1 6.95 us: from_everyone(): lax.all_to_all(jnp.broadcast_to(shard[None], (peers, *shard.shape)), axis...]
    dot_general x6 -> x0, matrix products: 7.25 us -> none  [the longest x1 4.12 us: local(): jnp.einsum('tl,td->ld', reordered, hidden_states, preferred_element_type=...]
  transfers between devices with their start and end apart: 2 -> 0, of which waited for: 2 -> 0; matrix products, arithmetic and copies ran while one was open for 1% -> 0% of each run, Pallas kernels for 0% -> 0%
where the time goes in v1:
time: 103 us; the launch traced here: 102 us
  Pallas kernels  96.2 us (93%)
  local copies, waits for them, and re-layouts  3.19 us (3%)
  other arithmetic  2.26 us (2%)
    pallas_call x1, Pallas kernels, local(): pl.pallas_call(kernel, out_shape=(jax.ShapeDtypeStruct((2, 32, BS), F32),...  96.2 us

profile of v1, /device:TPU:1, one launch (start us, length us, event | category | flops | bytes accessed | tf_op | source)
XLA Modules:
  0.0 102.4 jit_solution(4571076104810020265)
XLA Ops:
  0.6 0.0 copy-start
  0.6 0.0 copy-start.1
  0.7 0.7 multiply_add_fusion.2
  1.4 0.1 reshape.23
  1.4 0.1 copy.15
  1.6 0.1 reshape.24
  1.7 0.1 broadcast_in_dim.7
  1.7 0.6 broadcast_in_dim.8.slots
  2.3 96.2 %shard_map.103 = (f32[2,32,256]{2,1,0:T(8,128)}, f32[2,32,256]{2,1,0:T(8,128)}, f32[8,64,128]{2,1,0:T(8,128)}) custom-call(bf16[256,7168]{1,0:T(8,128)(2,1)} %hidden.1, bf16[256,512]{1,0:T(8,128)(2,1)} %latent.1, bf16[2,256,256]{2,1,0:T(8,128)(2,1)} %left_root.1, bf16[2,256,256]{2,1,0:T(8,128)(2,1)} %right_root.1, s32[8,64]{1,0:T(8,128)} %broadcast_in_dim.8.slots), custom_call_target="tpu_custom_call" | custom-call | tf_op jit(solution)/shard_map/pallas_call | solution.py:461
  98.6 0.0 copy-done
  98.6 0.0 copy-done.1
  98.6 1.5 %multiply_add_fusion = (f32[2,32,256]{2,1,0:T(8,128)}, f32[2,32,256]{2,1,0:T(8,128)}) fusion(f32[2,32,256]{2,1,0:T(8,128)} %get-tuple-element.7, f32[2,32,256]{2,1,0:T(8,128)S(1)} %copy-done, f32[2,32,256]{2,1,0:T(8,128)} %get-tuple-element.6, f32[2,32,256]{2,1,0:T(8,128)S(1)} %copy-done.1), kind=kLoop, calls=%fused_computation | loop fusion | flops 98304 | bytes 393216 | tf_op jit(solution)/shard_map/add | solution.py:476
  100.1 1.1 %copy.18 = f32[2,4,2,28,128]{4,2,3,1,0:T(2,128)S(1)} copy(f32[2,4,2,28,128]{4,3,2,1,0:T(8,128)} %bitcast.7) | data formatting | bytes 458752
  101.3 0.2 copy.17
  101.5 0.9 reshape.27
  (1 shorter events, 0.0 us)
Async XLA Ops:
  0.6 97.9 %copy-start = (f32[2,32,256]{2,1,0:T(8,128)S(1)}, f32[2,32,256]{2,1,0:T(8,128)}, u32[]{:S(2)}) copy-start(f32[2,32,256]{2,1,0:T(8,128)} %param.11) | copy-start | bytes 196612
  0.6 97.9 %copy-start.1 = (f32[2,32,256]{2,1,0:T(8,128)S(1)}, f32[2,32,256]{2,1,0:T(8,128)}, u32[]{:S(2)}) copy-start(f32[2,32,256]{2,1,0:T(8,128)} %param.10) | copy-start | bytes 196612

commit v2 on v1

v2 whole, which is shorter than its diff:
```python
import jax
import jax.numpy as jnp
from jax import lax
from jax.experimental import pallas as pl
from jax.experimental.pallas import tpu as pltpu
from jax.sharding import PartitionSpec as P

D = 7168
LAT = 512
BS = 256
TOK = 256
NX, NY, NZ = 4, 8, 8
NT = 8
HALF = 128
DECAY = 0.95
EPS = 1e-06

PAIRS = (("m", 6), ("x", 4), ("m", 4))
STARTS = tuple(sum(nj for _, nj in PAIRS[:k]) for k in range(len(PAIRS)))
PARTS = tuple(
    (group, first, start, nj)
    for (first, nj), start in zip(PAIRS, STARTS)
    for group in range(2)
)
SCHEDULE = (
    ("first", 0, 1),
    ("first", 1, 1),
    ("first", 2, 1),
    ("first", 0, 2),
    ("end", 1, 0),
    ("first", 2, 2),
    ("first", 0, 3),
    ("second", 1, 1),
    ("first", 2, 3),
    ("second", 1, 2),
    ("end", 0, 0),
    ("second", 1, 3),
    ("end", 2, 0),
    ("second", 0, 1),
    ("second", 2, 1),
    ("close", 1, 0),
    ("close", 0, 0),
    ("close", 2, 0),
)
FAR_FIRST = (4, 3, 5, 2, 6, 1, 7)
MESH = pl.DeviceIdType.MESH
F32 = jnp.float32
BF16 = jnp.bfloat16


def lanes_of(nj, d, step):
    cut = (nj + 1) // 2 * HALF
    if step > 0:
        return 0, nj * HALF
    return (0, cut) if d == 0 else (cut, nj * HALF)


def chain_shapes():
    shapes = {}
    for p, (_, first, _, nj) in enumerate(PARTS):
        for stage in range(2):
            over = first if stage == 0 else ("x" if first == "m" else "m")
            n = NX if over == "x" else 8
            for step in range(n // 2):
                for d in range(2):
                    if stage == 0:
                        rows = LAT // n // 2 if step == 0 else LAT // n
                        shapes[(p, stage, d, step)] = (rows, nj * HALF)
                    else:
                        low, high = lanes_of(nj, d, step)
                        shapes[(p, stage, d, step)] = (16, high - low)
    return shapes


CHAIN = chain_shapes()
KEYS = tuple(CHAIN)
INDEX = {key: k for k, key in enumerate(KEYS)}


def one_hot(rows, cols, match):
    r = lax.broadcasted_iota(jnp.int32, (rows, cols), 0)
    c = lax.broadcasted_iota(jnp.int32, (rows, cols), 1)
    return jnp.where(match(r, c), 1.0, 0.0).astype(BF16)


def mm(a, b, ca=1, cb=0):
    return lax.dot_general(a, b, (((ca,), (cb,)), ((), ())), preferred_element_type=F32)


def kernel(
    hidden, latent, left_factor, right_factor, left_root, right_root, owners, places,
    new_left, new_right, update, *scratch
):
    n = len(KEYS)
    sends, recvs, scratch = scratch[:n], scratch[n : 2 * n], scratch[2 * n :]
    np_ = len(PARTS)
    hc, scratch = scratch[:np_], scratch[np_:]
    prod, scratch = scratch[:np_], scratch[np_:]
    mid, scratch = scratch[:np_], scratch[np_:]
    (lat, lt, s3, r3, s2z, z2, s2x, x2, xs, yg, gf, s4z, s4b, z4, s5x, x4, upd,
     lf, rf, lroot, rroot,
     hsem, csem_s, csem_r, s3sem, a2a, psem) = scratch
    pend = []

    def send(copy):
        copy.start()
        pend.append(copy)

    y = lax.axis_index("replica")
    s = lax.axis_index("shard")
    xc = s % 8
    c = s % 2
    x = (s // 2) % 4
    z = s // 8

    ys = [(y + d) % 8 for d in range(8)]
    zs = [(z + d) % 8 for d in range(8)]
    cs = [(xc + d) % 8 for d in range(8)]
    xn = [(x + d) % 4 for d in range(4)]

    def dev(xx=None, yy=None, zz=None, xcc=None):
        q = xc if xcc is None else xcc
        if xx is not None:
            q = xx * 2 + c
        return (y if yy is None else yy, (z if zz is None else zz) * 8 + q)

    partner = dev(xcc=x * 2 + (1 - c))

    def columns(p, core):
        group, _, start, nj = PARTS[p]
        at = (group * 14 + start) * BS + core * (nj * HALF)
        return hidden.at[:, pl.ds(pl.multiple_of(at, HALF), nj * HALF)]

    def all_own(p):
        return pltpu.make_async_copy(columns(p, c), hc[p].at[pl.ds(0, TOK), :], hsem.at[0, p])

    def all_far(p):
        return pltpu.make_async_remote_copy(
            columns(p, 1 - c), hc[p].at[pl.ds(TOK, TOK), :],
            hsem.at[1, p], hsem.at[2, p], device_id=partner, device_id_type=MESH,
        )

    own_lat = pltpu.make_async_copy(latent, lat.at[0], hsem.at[0, np_])
    far_lat = pltpu.make_async_remote_copy(
        latent, lat.at[1], hsem.at[1, np_], hsem.at[2, np_],
        device_id=partner, device_id_type=MESH,
    )
    own_lat.start()
    params = [
        pltpu.make_async_copy(src, dst, psem.at[k])
        for k, (src, dst) in enumerate(
            ((left_root, lroot), (right_root, rroot), (left_factor, lf), (right_factor, rf))
        )
    ]
    for p in range(np_):
        all_own(p).start()
    for k in params:
        k.start()

    barrier = pltpu.get_barrier_semaphore()
    for d in FAR_FIRST:
        for to in (dev(yy=ys[d]), dev(zz=zs[d]), dev(xcc=cs[d])):
            pl.semaphore_signal(barrier, inc=1, device_id=to, device_id_type=MESH)
    pl.semaphore_wait(barrier, 21)

    send(far_lat)
    for p in range(np_):
        send(all_far(p))

    perm_a = one_hot(LAT, LAT, lambda r, k: k == (r % 2) * BS + r // 2)
    perm_b = one_hot(
        LAT, LAT,
        lambda r, k: k == (r % 2) * BS + (r // 128) * 64 + ((r // 2) % 8) * 8 + (r // 16) % 8,
    )
    own_lat.wait()
    lt[0, :, 0:TOK] = mm(perm_a, lat[0], 1, 1).astype(BF16)
    lt[1, :, 0:TOK] = mm(perm_b, lat[0], 1, 1).astype(BF16)
    far_lat.wait_recv()
    lt[0, :, TOK : 2 * TOK] = mm(perm_a, lat[1], 1, 1).astype(BF16)
    lt[1, :, TOK : 2 * TOK] = mm(perm_b, lat[1], 1, 1).astype(BF16)

    def axis_of(p, stage):
        group, first, _, _ = PARTS[p]
        over = first if stage == 0 else ("x" if first == "m" else "m")
        if over == "x":
            return 4, xn, lambda v: dev(xx=v)
        if group == 0:
            return 8, ys, lambda v: dev(yy=v)
        return 8, zs, lambda v: dev(zz=v)

    def copy_of(p, stage, d, step):
        num, me, at = axis_of(p, stage)
        k = INDEX[(p, stage, d, step)]
        to = me[1] if d == 0 else me[num - 1]
        return pltpu.make_async_remote_copy(
            sends[k], recvs[k], csem_s.at[k], csem_r.at[k],
            device_id=at(to), device_id_type=MESH,
        )

    def own_rows(p, chunk, piece):
        if PARTS[p][1] == "x":
            start = chunk * 128 + piece * 16
        else:
            start = piece * 128 + chunk * 16
        return prod[p][pl.ds(pl.multiple_of(start, 16), 16), :]

    def chunk_of(p, stage, d, step):
        num, me, _ = axis_of(p, stage)
        far_by = num // 2 - step
        return me[far_by] if d == 0 else me[num - far_by]

    def rows16(i):
        if not isinstance(i, int):
            i = pl.multiple_of(i * 16, 16)
            return pl.ds(i, 16)
        return pl.ds(i * 16, 16)

    def send_first(p, step):
        rows = LAT // axis_of(p, 0)[0] // 16
        for d in range(2):
            k = INDEX[(p, 0, d, step)]
            chunk = chunk_of(p, 0, d, step)
            half = (0, rows // 2) if d == 0 else (rows // 2, rows)
            rest = (rows // 2, rows) if d == 0 else (0, rows // 2)

            def emit(span, base, prev=None, prev_base=0):
                for i in range(*span):
                    value = own_rows(p, chunk, i)
                    if prev is not None:
                        value = value + prev[rows16(i - prev_base), :].astype(F32)
                    sends[k][rows16(i - base), :] = value.astype(BF16)

            if step == 0:
                emit(half, half[0])
            else:
                if step == 1:
                    emit(rest, 0)
                copy_of(p, 0, d, step - 1).wait_recv()
                prev = recvs[INDEX[(p, 0, d, step - 1)]]
                if step == 1:
                    emit(half, 0, prev, half[0])
                else:
                    emit((0, rows), 0, prev)
            send(copy_of(p, 0, d, step))

    def finish_first(p):
        num, me, _ = axis_of(p, 0)
        last = num // 2 - 1
        for d in range(2):
            copy_of(p, 0, d, last).wait_recv()
        up = recvs[INDEX[(p, 0, 0, last)]]
        down = recvs[INDEX[(p, 0, 1, last)]]

        for i in range(LAT // num // 16):
            at = rows16(i)
            mid[p][at, :] = own_rows(p, me[0], i) + up[at, :].astype(F32) + down[at, :].astype(F32)

    def send_second(p, step):
        nj = PARTS[p][3]
        for d in range(2):
            k = INDEX[(p, 1, d, step)]
            at = rows16(chunk_of(p, 1, d, step))
            kind = sends[k].dtype
            if step == 0:
                low, high = lanes_of(nj, d, 0)
                sends[k][...] = mid[p][at, low:high].astype(kind)
            else:
                copy_of(p, 1, d, step - 1).wait_recv()
                prev = recvs[INDEX[(p, 1, d, step - 1)]]
                if step == 1:
                    for e in range(2):
                        low, high = lanes_of(nj, e, 0)
                        value = mid[p][at, low:high]
                        if e == d:
                            value = value + prev[...].astype(F32)
                        sends[k][:, low:high] = value.astype(kind)
                else:
                    sends[k][...] = (mid[p][at, :] + prev[...].astype(F32)).astype(kind)
            send(copy_of(p, 1, d, step))

    def finish_second(p):
        num, me, _ = axis_of(p, 1)
        last = num // 2 - 1
        for d in range(2):
            copy_of(p, 1, d, last).wait_recv()
        up = recvs[INDEX[(p, 1, 0, last)]]
        down = recvs[INDEX[(p, 1, 1, last)]]
        group, _, j0, nj = PARTS[p]
        total = mid[p][rows16(me[0]), :] + up[...].astype(F32) + down[...].astype(F32)
        for k in range(nj):
            row = 2 * (j0 + k)
            for t in range(8):
                s3[group, t, row : row + 2, :] = total[
                    2 * t : 2 * t + 2, k * HALF : (k + 1) * HALF
                ]

    for p in range(np_):
        all_own(p).wait()
        all_far(p).wait_recv()
        group, _, _, nj = PARTS[p]
        prod[p][...] = mm(lt[group], hc[p][...])
        send_first(p, 0)

    s3[:, :, 28:32, :] = jnp.zeros((2, 8, 4, HALF), F32)
    for event, pair, step in SCHEDULE:
        for p in (2 * pair, 2 * pair + 1):
            if event == "first":
                send_first(p, step)
            elif event == "end":
                finish_first(p)
                send_second(p, 0)
            elif event == "second":
                send_second(p, step)
            else:
                finish_second(p)
    def s3_copy(group, d):
        to = zs[d] if group == 0 else ys[d]
        return pltpu.make_async_remote_copy(
            s3.at[group, to], r3.at[group, d - 1],
            s3sem.at[0, group, d - 1], s3sem.at[1, group, d - 1],
            device_id=dev(zz=to) if group == 0 else dev(yy=to), device_id_type=MESH,
        )

    for group in range(2):
        for d in FAR_FIRST:
            send(s3_copy(group, d))
    pieces = []
    for group in range(2):
        total = s3[group, z if group == 0 else y]
        for d in (1, 7, 2, 6, 3, 5, 4):
            s3_copy(group, d).wait_recv()
            total = total + r3[group, d - 1]
        pieces.append(total)
    piece = jnp.concatenate(pieces, axis=0).astype(BF16)

    def exchange(k, src, dst, me, at, whole=False):
        return [
            pltpu.make_async_remote_copy(
                src if whole else src.at[me[d]],
                dst.at[me[0]],
                a2a.at[k, 0, d - 1], a2a.at[k, 1, d - 1],
                device_id=at(me[d]), device_id_type=MESH,
            )
            for d in FAR_FIRST
        ]

    kk = lax.broadcasted_iota(jnp.int32, (8, 64), 1) % 32 // 2
    col = kk
    for (_, nj), start in zip(PAIRS, STARTS):
        inside = (kk >= start) & (kk < start + nj)
        col = jnp.where(inside, start + c * (nj // 2) + (kk - start) // 2, col)
    lane = lax.broadcasted_iota(jnp.int32, (8, 64), 1)
    block = jnp.where(kk < 14, (lane % 2) * 28 + (lane // 32) * 14 + col, -1)[0:1, :]
    to_rows = jnp.where(
        lax.broadcasted_iota(jnp.int32, (56, 64), 0) == block, 1.0, 0.0
    ).astype(BF16)
    flat = (owners[...] * 2 + places[...] + 1).astype(F32).astype(BF16)
    half_row = (mm(flat, to_rows).astype(jnp.int32) - 1) * 2 + kk[0:1, :] % 2
    dispatch = jnp.where(
        lax.broadcasted_iota(jnp.int32, (BS, 64), 0) == half_row, 1.0, 0.0
    ).astype(BF16)
    regroup = one_hot(
        BS, BS,
        lambda o, i: i == (o % 8) * 32 + (o // 32) * 4 + (o // 16) % 2 * 2 + (o // 8) % 2,
    )
    s2z[...] = mm(dispatch, piece).astype(BF16).reshape(8, 32, HALF)
    ex = exchange(0, s2z, z2, zs, lambda v: dev(zz=v))
    for k in ex:
        send(k)
    z2[z] = s2z[z]
    for k in ex:
        k.wait_recv()
    s2x[...] = mm(regroup, z2[...].reshape(BS, HALF)).astype(BF16).reshape(8, 32, HALF)
    ex2 = exchange(1, s2x, x2, cs, lambda v: dev(xcc=v))
    for k in ex2:
        send(k)
    x2[xc] = s2x[xc]
    for k in ex2:
        k.wait_recv()
    for q in range(4):
        xs[q] = (x2[2 * q].astype(F32) + x2[2 * q + 1].astype(F32)).astype(BF16)
    ex3 = exchange(2, xs, yg, ys, lambda v: dev(yy=v), whole=True)
    for k in ex3:
        send(k)
    yg[y] = xs[...]
    for k in ex3:
        k.wait_recv()
    for yy in range(8):
        for q in range(4):
            rows = yg[yy, q].astype(F32)
            for k in range(4):
                gf[
                    k // 2,
                    q * 64 + yy * 8 : q * 64 + yy * 8 + 8,
                    (k % 2) * HALF : (k % 2 + 1) * HALF,
                ] = rows[k * 8 : k * 8 + 8, :]

    for k in params:
        k.wait()
    pick_rows = one_hot(64, BS, lambda r, k: k == r * 4 + y % 4)
    lane_half = pl.ds(pl.multiple_of((y // 4) * HALF, HALF), HALF)
    for slot in range(2):
        g = gf[slot]
        product = mm(lroot[slot], g.astype(BF16))
        half = product.astype(BF16)
        low = (product - half.astype(F32)).astype(BF16)
        root = rroot[slot]
        shaped = mm(half, root) + mm(low, root)
        grad_scale = jnp.sqrt(jnp.sum(g * g, keepdims=True) * (1.0 / (BS * BS)))
        shaped_scale = jnp.sqrt(jnp.sum(shaped * shaped, keepdims=True) * (1.0 / (BS * BS)) + EPS)
        root = rroot[slot, :, lane_half]
        chosen = mm(mm(pick_rows, half).astype(BF16), root) + mm(mm(pick_rows, low).astype(BF16), root)
        back = chosen * (grad_scale / shaped_scale)
        s4z[:, slot * 8 : slot * 8 + 8, :] = back.reshape(8, 8, HALF)
    s4b[...] = s4z[...].astype(BF16)
    ex4 = exchange(3, s4b, z4, zs, lambda v: dev(zz=v))
    for k in ex4:
        send(k)
    z4[z] = s4b[z]

    rows_here = one_hot(32, BS, lambda r, k: k == r + y * 32)
    for slot in range(2):
        g = gf[slot].astype(BF16)
        new_left[slot] = DECAY * lf[slot] + (1.0 - DECAY) * mm(mm(rows_here, g).astype(BF16), g, 1, 1)
        new_right[slot] = DECAY * rf[slot] + (1.0 - DECAY) * mm(mm(rows_here, g, 1, 1).astype(BF16), g)
    regroup_back = one_hot(
        128, 128, lambda o, i: i == ((o // 2) % 8) * 16 + (o % 2) * 8 + o // 16
    )
    lane = lax.broadcasted_iota(jnp.int32, (8, 64), 1)
    block = jnp.where(lane < 56, lane, -1)[0:1, :]
    wide = jnp.where(
        lax.broadcasted_iota(jnp.int32, (56, 64), 0) == block, 1.0, 0.0
    ).astype(BF16)
    slot_row = mm(flat, wide).astype(jnp.int32) - 1
    owner = slot_row // 2
    back_slot = jnp.where(slot_row < 0, -1, (owner % 8) * 16 + (owner // 8) * 2 + slot_row % 2)
    picker = jnp.where(
        lax.broadcasted_iota(jnp.int32, (128, 64), 0) == back_slot, 1.0, 0.0
    ).astype(BF16)
    spread = one_hot(512, BS, lambda o, i: (o % 8 < 4) & (i == (o % 8) * 64 + o // 8))

    for k in ex4:
        k.wait_recv()
    s5x[...] = mm(regroup_back, z4[...].reshape(128, HALF)).astype(BF16).reshape(8, 16, HALF)
    ex5 = exchange(4, s5x, x4, cs, lambda v: dev(xcc=v))
    for k in ex5:
        send(k)
    x4[xc] = s5x[xc]
    for k in ex5:
        k.wait_recv()
    upd[y] = mm(picker, x4[...].reshape(128, HALF), 0, 0).astype(BF16)
    ex6 = exchange(5, upd.at[y], upd, ys, lambda v: dev(yy=v), whole=True)
    for k in ex6:
        send(k)
    for k in ex6:
        k.wait_recv()
    for h in range(2):
        tiles = mm(spread, upd[4 * h : 4 * h + 4].reshape(256, HALF))
        for j in range(28):
            for i in range(2):
                row = i * 28 + j
                update[i, :, j * BS + h * HALF : j * BS + (h + 1) * HALF] = tiles[
                    row * 8 : row * 8 + 4, :
                ]

    for k in pend:
        k.wait_send()


def move(a, b, c, to_a, to_b, to_c):
    to_a[...] = a[...]
    to_b[...] = b[...]
    to_c[...] = c[...]


def local(
    hidden_states,
    latent_grad,
    left_factor,
    right_factor,
    left_root,
    right_root,
    block_owner,
    block_slot,
):
    dtype_of = lambda key: BF16 if key[1] == 0 or PARTS[key[0]][1] == "m" else F32
    bufs = [pltpu.VMEM(CHAIN[key], dtype_of(key)) for key in KEYS]
    scratch = bufs + bufs
    for width_of in (lambda w: ((2 * TOK, w), BF16), lambda w: ((LAT, w), F32)):
        scratch = scratch + [pltpu.VMEM(*width_of(part[3] * HALF)) for part in PARTS]
    scratch = scratch + [
        pltpu.VMEM((128 if part[1] == "x" else 64, part[3] * HALF), F32) for part in PARTS
    ]
    scratch = scratch + [
        pltpu.VMEM((2, TOK, LAT), BF16),
        pltpu.VMEM((2, LAT, 2 * TOK), BF16),
        pltpu.VMEM((2, 8, 32, HALF), F32),
        pltpu.VMEM((2, 7, 32, HALF), F32),
        pltpu.VMEM((8, 32, HALF), BF16),
        pltpu.VMEM((8, 32, HALF), BF16),
        pltpu.VMEM((8, 32, HALF), BF16),
        pltpu.VMEM((8, 32, HALF), BF16),
        pltpu.VMEM((4, 32, HALF), BF16),
        pltpu.VMEM((8, 4, 32, HALF), BF16),
        pltpu.VMEM((2, BS, BS), F32),
        pltpu.VMEM((8, 16, HALF), F32),
        pltpu.VMEM((8, 16, HALF), BF16),
        pltpu.VMEM((8, 16, HALF), BF16),
        pltpu.VMEM((8, 16, HALF), BF16),
        pltpu.VMEM((8, 16, HALF), BF16),
        pltpu.VMEM((8, 64, HALF), BF16),
        pltpu.VMEM((2, 32, BS), F32),
        pltpu.VMEM((2, 32, BS), F32),
        pltpu.VMEM((2, BS, BS), BF16),
        pltpu.VMEM((2, BS, BS), BF16),
        pltpu.SemaphoreType.DMA((3, len(PARTS) + 1)),
        pltpu.SemaphoreType.DMA((len(KEYS),)),
        pltpu.SemaphoreType.DMA((len(KEYS),)),
        pltpu.SemaphoreType.DMA((2, 2, 7)),
        pltpu.SemaphoreType.DMA((6, 2, 7)),
        pltpu.SemaphoreType.DMA((4,)),
    ]
    vmem = pl.BlockSpec(memory_space=pltpu.VMEM)
    anywhere = pl.BlockSpec(memory_space=pl.ANY)
    results = pl.pallas_call(
        kernel,
        out_shape=(
            jax.ShapeDtypeStruct((2, 32, BS), F32),
            jax.ShapeDtypeStruct((2, 32, BS), F32),
            jax.ShapeDtypeStruct((2, 4, D), F32),
        ),
        in_specs=[anywhere] * 6 + [vmem, vmem],
        out_specs=(vmem, vmem, vmem),
        scratch_shapes=scratch,
        compiler_params=pltpu.CompilerParams(
            collective_id=0, has_side_effects=True, vmem_limit_bytes=56 * 1024 * 1024
        ),
    )(
        hidden_states,
        latent_grad,
        left_factor,
        right_factor,
        left_root,
        right_root,
        block_owner.reshape(1, 56),
        block_slot.reshape(1, 56),
    )
    return pl.pallas_call(
        move,
        out_shape=tuple(jax.ShapeDtypeStruct(r.shape, r.dtype) for r in results),
        in_specs=[vmem] * 3,
        out_specs=(vmem,) * 3,
    )(*results)


def solution(mesh):
    placed = (
        P(("replica", "shard"), None),
        P(("replica", "shard"), None),
        P("shard", "replica", None),
        P("shard", "replica", None),
        P("shard", None, None),
        P("shard", None, None),
        P(),
        P(),
    )
    return jax.shard_map(
        local,
        mesh=mesh,
        in_specs=placed,
        out_specs=(
            P("shard", "replica", None),
            P("shard", "replica", None),
            P(None, "shard", None),
        ),
        check_vma=False,
    )
```

time: 103 us -> 92.8 us (0.901)
  Pallas kernels: 96.2 us -> 92 us
  local copies, waits for them, and re-layouts: 3.19 us -> 0 us
  other arithmetic: 2.26 us -> 0 us
    pallas_call x1, Pallas kernels: 96.2 us -> 90.3 us  [local(): pl.pallas_call(kernel, out_shape=(jax.ShapeDtypeStruct((2, 32, BS), F32),...]
    add x2 -> x0, other arithmetic: 2.26 us -> none  [the longest x1 1.55 us: local(): new_right = DECAY * right_factor + (1.0 - DECAY) * ggr]
    pallas_call x0 -> x1, Pallas kernels: none -> 1.74 us  [local(): pl.pallas_call(move, out_shape=tuple((jax.ShapeDtypeStruct(r.shape, r.dty...]
    unnamed x5 -> x0, local copies, waits for them, and re-layouts: 1.14 us -> none
    reshape x3 -> x0, local copies, waits for them, and re-layouts: 1.08 us -> none  [the longest x1 0.91 us: local(): update = upd.reshape(2, 4, 2, 32, HALF)[:, :, :, :28].reshape(2, 4, 2, 14...]
where the time goes in v2:
time: 92.8 us; the launch traced here: 92.7 us
  Pallas kernels  92 us (99%)
    pallas_call x1, Pallas kernels, local(): pl.pallas_call(kernel, out_shape=(jax.ShapeDtypeStruct((2, 32, BS), F32),...  90.3 us

profile of v2, /device:TPU:1, one launch (start us, length us, event | category | flops | bytes accessed | tf_op | source)
XLA Modules:
  0.0 92.7 jit_solution(13870786830490839757)
XLA Ops:
  0.6 90.3 %shard_map.103 = (f32[2,32,256]{2,1,0:T(8,128)}, f32[2,32,256]{2,1,0:T(8,128)}, f32[2,4,7168]{2,1,0:T(4,128)}) custom-call(bf16[256,7168]{1,0:T(8,128)(2,1)} %hidden.1, bf16[256,512]{1,0:T(8,128)(2,1)} %latent.1, f32[2,32,256]{2,1,0:T(8,128)} %left_factor.1, f32[2,32,256]{2,1,0:T(8,128)} %right_factor.1, bf16[2,256,256]{2,1,0:T(8,128)(2,1)} %left_root.1, ...), custom_call_target="tpu_custom_call" | custom-call | tf_op jit(solution)/shard_map/pallas_call | solution.py:525
  90.9 1.7 %shard_map.104 = (f32[2,32,256]{2,1,0:T(8,128)}, f32[2,32,256]{2,1,0:T(8,128)}, f32[2,4,7168]{2,1,0:T(4,128)}) custom-call(f32[2,32,256]{2,1,0:T(8,128)} %get-tuple-element.6.a, f32[2,32,256]{2,1,0:T(8,128)} %get-tuple-element.7.b, f32[2,4,7168]{2,1,0:T(4,128)} %get-tuple-element.8.c), custom_call_target="tpu_custom_call" | custom-call | tf_op jit(solution)/shard_map/pallas_call | solution.py:548

commit v3 on v2

--- a/solution.py
+++ b/solution.py
@@ -15,7 +15,7 @@
 DECAY = 0.95
 EPS = 1e-06
 
-PAIRS = (("m", 6), ("x", 4), ("m", 4))
+PAIRS = (("m", 6), ("x", 2), ("m", 6))
 STARTS = tuple(sum(nj for _, nj in PAIRS[:k]) for k in range(len(PAIRS)))
 PARTS = tuple(
     (group, first, start, nj)
@@ -30,11 +30,8 @@
     ("end", 1, 0),
     ("first", 2, 2),
     ("first", 0, 3),
-    ("second", 1, 1),
     ("first", 2, 3),
-    ("second", 1, 2),
     ("end", 0, 0),
-    ("second", 1, 3),
     ("end", 2, 0),
     ("second", 0, 1),
     ("second", 2, 1),
@@ -58,7 +55,7 @@
 def chain_shapes():
     shapes = {}
     for p, (_, first, _, nj) in enumerate(PARTS):
-        for stage in range(2):
+        for stage in range(1 if first == "x" else 2):
             over = first if stage == 0 else ("x" if first == "m" else "m")
             n = NX if over == "x" else 8
             for step in range(n // 2):
@@ -98,13 +95,18 @@
     prod, scratch = scratch[:np_], scratch[np_:]
     mid, scratch = scratch[:np_], scratch[np_:]
     (lat, lt, s3, r3, s2z, z2, s2x, x2, xs, yg, gf, s4z, s4b, z4, s5x, x4, upd,
-     lf, rf, lroot, rroot,
-     hsem, csem_s, csem_r, s3sem, a2a, psem) = scratch
+     lf, rf, lroot, rroot, d2, e2,
+     hsem, csem_s, csem_r, s3sem, a2a, psem, s2sem) = scratch
     pend = []
 
     def send(copy):
         copy.start()
         pend.append(copy)
+
+    def settle(count):
+        for copy in pend[:count]:
+            copy.wait_send()
+        del pend[:count]
 
     y = lax.axis_index("replica")
     s = lax.axis_index("shard")
@@ -145,6 +147,10 @@
         latent, lat.at[1], hsem.at[1, np_], hsem.at[2, np_],
         device_id=partner, device_id_type=MESH,
     )
+    barrier = pltpu.get_barrier_semaphore()
+    for d in FAR_FIRST:
+        for to in (dev(yy=ys[d]), dev(zz=zs[d]), dev(xcc=cs[d])):
+            pl.semaphore_signal(barrier, inc=1, device_id=to, device_id_type=MESH)
     own_lat.start()
     params = [
         pltpu.make_async_copy(src, dst, psem.at[k])
@@ -157,16 +163,6 @@
     for k in params:
         k.start()
 
-    barrier = pltpu.get_barrier_semaphore()
-    for d in FAR_FIRST:
-        for to in (dev(yy=ys[d]), dev(zz=zs[d]), dev(xcc=cs[d])):
-            pl.semaphore_signal(barrier, inc=1, device_id=to, device_id_type=MESH)
-    pl.semaphore_wait(barrier, 21)
-
-    send(far_lat)
-    for p in range(np_):
-        send(all_far(p))
-
     perm_a = one_hot(LAT, LAT, lambda r, k: k == (r % 2) * BS + r // 2)
     perm_b = one_hot(
         LAT, LAT,
@@ -175,6 +171,12 @@
     own_lat.wait()
     lt[0, :, 0:TOK] = mm(perm_a, lat[0], 1, 1).astype(BF16)
     lt[1, :, 0:TOK] = mm(perm_b, lat[0], 1, 1).astype(BF16)
+    pl.semaphore_wait(barrier, 21)
+
+    send(far_lat)
+    for p in range(np_):
+        send(all_far(p))
+
     far_lat.wait_recv()
     lt[0, :, TOK : 2 * TOK] = mm(perm_a, lat[1], 1, 1).astype(BF16)
     lt[1, :, TOK : 2 * TOK] = mm(perm_b, lat[1], 1, 1).astype(BF16)
@@ -254,6 +256,20 @@
         for i in range(LAT // num // 16):
             at = rows16(i)
             mid[p][at, :] = own_rows(p, me[0], i) + up[at, :].astype(F32) + down[at, :].astype(F32)
+
+    def direct(p, d):
+        group = PARTS[p][0]
+        _, me, at = axis_of(p, 1)
+        return pltpu.make_async_remote_copy(
+            d2.at[group, rows16(me[d])], e2.at[group, d - 1],
+            s2sem.at[0, group, d - 1], s2sem.at[1, group, d - 1],
+            device_id=at(me[d]), device_id_type=MESH,
+        )
+
+    def send_direct(p):
+        d2[PARTS[p][0]] = mid[p][...].astype(BF16)
+        for d in FAR_FIRST:
+            send(direct(p, d))
 
     def send_second(p, step):
         nj = PARTS[p][3]
@@ -280,13 +296,17 @@
 
     def finish_second(p):
         num, me, _ = axis_of(p, 1)
-        last = num // 2 - 1
-        for d in range(2):
-            copy_of(p, 1, d, last).wait_recv()
-        up = recvs[INDEX[(p, 1, 0, last)]]
-        down = recvs[INDEX[(p, 1, 1, last)]]
-        group, _, j0, nj = PARTS[p]
-        total = mid[p][rows16(me[0]), :] + up[...].astype(F32) + down[...].astype(F32)
+        group, first, j0, nj = PARTS[p]
+        total = mid[p][rows16(me[0]), :]
+        if first == "x":
+            for d in FAR_FIRST[::-1]:
+                direct(p, d).wait_recv()
+                total = total + e2[group, d - 1].astype(F32)
+        else:
+            last = num // 2 - 1
+            for d in range(2):
+                copy_of(p, 1, d, last).wait_recv()
+                total = total + recvs[INDEX[(p, 1, d, last)]][...].astype(F32)
         for k in range(nj):
             row = 2 * (j0 + k)
             for t in range(8):
@@ -308,7 +328,10 @@
                 send_first(p, step)
             elif event == "end":
                 finish_first(p)
-                send_second(p, 0)
+                if PARTS[p][1] == "x":
+                    send_direct(p)
+                else:
+                    send_second(p, 0)
             elif event == "second":
                 send_second(p, step)
             else:
@@ -324,6 +347,7 @@
     for group in range(2):
         for d in FAR_FIRST:
             send(s3_copy(group, d))
+    settle(len(pend) - 44)
     pieces = []
     for group in range(2):
         total = s3[group, z if group == 0 else y]
@@ -367,6 +391,7 @@
     ex = exchange(0, s2z, z2, zs, lambda v: dev(zz=v))
     for k in ex:
         send(k)
+    settle(len(pend) - 21)
     z2[z] = s2z[z]
     for k in ex:
         k.wait_recv()
@@ -374,6 +399,7 @@
     ex2 = exchange(1, s2x, x2, cs, lambda v: dev(xcc=v))
     for k in ex2:
         send(k)
+    settle(len(pend) - 7)
     x2[xc] = s2x[xc]
     for k in ex2:
         k.wait_recv()
@@ -382,6 +408,7 @@
     ex3 = exchange(2, xs, yg, ys, lambda v: dev(yy=v), whole=True)
     for k in ex3:
         send(k)
+    settle(len(pend) - 7)
     yg[y] = xs[...]
     for k in ex3:
         k.wait_recv()
@@ -416,6 +443,7 @@
     ex4 = exchange(3, s4b, z4, zs, lambda v: dev(zz=v))
     for k in ex4:
         send(k)
+    settle(len(pend) - 7)
     z4[z] = s4b[z]
 
     rows_here = one_hot(32, BS, lambda r, k: k == r + y * 32)
@@ -445,6 +473,7 @@
     ex5 = exchange(4, s5x, x4, cs, lambda v: dev(xcc=v))
     for k in ex5:
         send(k)
+    settle(len(pend) - 7)
     x4[xc] = s5x[xc]
     for k in ex5:
         k.wait_recv()
@@ -452,6 +481,7 @@
     ex6 = exchange(5, upd.at[y], upd, ys, lambda v: dev(yy=v), whole=True)
     for k in ex6:
         send(k)
+    settle(len(pend) - 7)
     for k in ex6:
         k.wait_recv()
     for h in range(2):
@@ -484,6 +514,7 @@
     block_slot,
 ):
     dtype_of = lambda key: BF16 if key[1] == 0 or PARTS[key[0]][1] == "m" else F32
+    wide = sum(nj for first, nj in PAIRS if first == "x") * HALF
     bufs = [pltpu.VMEM(CHAIN[key], dtype_of(key)) for key in KEYS]
     scratch = bufs + bufs
     for width_of in (lambda w: ((2 * TOK, w), BF16), lambda w: ((LAT, w), F32)):
@@ -513,12 +544,15 @@
         pltpu.VMEM((2, 32, BS), F32),
         pltpu.VMEM((2, BS, BS), BF16),
         pltpu.VMEM((2, BS, BS), BF16),
+        pltpu.VMEM((2, 128, wide), BF16),
+        pltpu.VMEM((2, 7, 16, wide), BF16),
         pltpu.SemaphoreType.DMA((3, len(PARTS) + 1)),
         pltpu.SemaphoreType.DMA((len(KEYS),)),
         pltpu.SemaphoreType.DMA((len(KEYS),)),
         pltpu.SemaphoreType.DMA((2, 2, 7)),
         pltpu.SemaphoreType.DMA((6, 2, 7)),
         pltpu.SemaphoreType.DMA((4,)),
+        pltpu.SemaphoreType.DMA((2, 2, 7)),
     ]
     vmem = pl.BlockSpec(memory_space=pltpu.VMEM)
     anywhere = pl.BlockSpec(memory_space=pl.ANY)

time: 92.8 us -> 88.7 us (0.956)
  Pallas kernels: 92 us -> 87.9 us
    pallas_call x1, Pallas kernels: 90.3 us -> 86.2 us  [local(): pl.pallas_call(kernel, out_shape=(jax.ShapeDtypeStruct((2, 32, BS), F32),...]
where the time goes in v3:
time: 88.7 us; the launch traced here: 88.6 us
  Pallas kernels  87.9 us (99%)
    pallas_call x1, Pallas kernels, local(): pl.pallas_call(kernel, out_shape=(jax.ShapeDtypeStruct((2, 32, BS), F32),...  86.2 us

profile of v3, /device:TPU:1, one launch (start us, length us, event | category | flops | bytes accessed | tf_op | source)
XLA Modules:
  0.0 88.6 jit_solution(2137644886183880354)
XLA Ops:
  0.6 86.2 %shard_map.103 = (f32[2,32,256]{2,1,0:T(8,128)}, f32[2,32,256]{2,1,0:T(8,128)}, f32[2,4,7168]{2,1,0:T(4,128)}) custom-call(bf16[256,7168]{1,0:T(8,128)(2,1)} %hidden.1, bf16[256,512]{1,0:T(8,128)(2,1)} %latent.1, f32[2,32,256]{2,1,0:T(8,128)} %left_factor.1, f32[2,32,256]{2,1,0:T(8,128)} %right_factor.1, bf16[2,256,256]{2,1,0:T(8,128)(2,1)} %left_root.1, ...), custom_call_target="tpu_custom_call" | custom-call | tf_op jit(solution)/shard_map/pallas_call | solution.py:559
  86.8 1.7 %shard_map.104 = (f32[2,32,256]{2,1,0:T(8,128)}, f32[2,32,256]{2,1,0:T(8,128)}, f32[2,4,7168]{2,1,0:T(4,128)}) custom-call(f32[2,32,256]{2,1,0:T(8,128)} %get-tuple-element.6.a, f32[2,32,256]{2,1,0:T(8,128)} %get-tuple-element.7.b, f32[2,4,7168]{2,1,0:T(4,128)} %get-tuple-element.8.c), custom_call_target="tpu_custom_call" | custom-call | tf_op jit(solution)/shard_map/pallas_call | solution.py:582
